TPU v7x, 128 devices: a whole 4x4x4 slice. The times are simulated.
128 devices in a mesh: blk: 64 (over z, y_lo, x, core), band: 2 (over y_hi).
Axes of the slice: x: 4, y: 4 (y_hi: 2, y_lo: 2; y = y_hi * 2 + y_lo), z: 4, core: 2. Of those that a mesh axis runs over, the one named last changes fastest.
Arguments:
- traces: bfloat16 [2048, 4096], P('blk'), may hold values from -6 to 6
- pair_list: int32 [16384, 2], P(('blk', 'band')), may hold values from 0 to 95, as said below
- counts: int32 [128], P(('blk', 'band')), may hold values from 16 to 128, as said below
- band_edges: int32 [4], replicated, may hold values from 1 to 2048, as said below
- observed: float32 [16384, 3, 512], P(('blk', 'band')), may hold values from -6 to 6
Outputs:
- adjoint: float32 [2048, 4096], P('blk', 'band')
- misfit: float32 [16384], P(('blk', 'band'))
Inputs may be any that keep to these rules, and one draw needn't show every extreme that they name: pair_list[p, 0] < 32 and pair_list[p, 1] < 96; pair_list[p, 1] // 32 says whether the second channel lies in the owning block or one or two blocks before it on the cycle. `counts`: at most 128 used slots on a device, the used slots first; some device uses all 128. The edges rise strictly; band n covers bins band_edges[n] to band_edges[n + 1] - 1; the last edge is 2048.
All inputs are finite; a program needn't handle non-finite values.
Results may differ from a plain program's by a relative error of at most 0.011.
Values may be sent and summed in bfloat16 or wider, within the bound.
A program may use at most 192 MiB of HBM per device.

v0:
```python
import functools
import math

import jax
import jax.numpy as jnp
import ml_dtypes
import numpy as np
from jax import lax
from jax.experimental import pallas as pl
from jax.experimental.pallas import tpu as pltpu
from jax.sharding import PartitionSpec as P

SAMPLES = 4096
FREQ_BINS = 2048
MAX_LAG = 256
LAGS = 2 * MAX_LAG
BANDS = 3
CHAN = 32
PAIRS = 128
EPSILON = 1e-05
N1 = 16
N2 = 256
F2 = FREQ_BINS // N1
CHUNKS = 4
PER = N1 // CHUNKS
MESH = pl.DeviceIdType.MESH


def lag_table():
    f = np.arange(N1)[:, None] + N1 * np.arange(F2)[None, :]
    shift = np.arange(-MAX_LAG, MAX_LAG)
    angle = np.mod(f[:, :, None] * shift, SAMPLES) * (2.0 * np.pi / SAMPLES)
    rows = np.stack([np.cos(angle), -np.sin(angle)], axis=1) / math.sqrt(FREQ_BINS / 8.0)
    return rows.reshape(N1, 2 * F2, LAGS).astype(ml_dtypes.bfloat16)


def dft_table():
    angle = np.mod(np.arange(N2)[:, None] * np.arange(F2)[None, :], N2) * (2.0 * np.pi / N2)
    c, s = np.cos(angle), np.sin(angle)
    return np.block([[c, -s], [s, c]])


def twiddles():
    angle = np.arange(N1)[:, None] * np.arange(N2)[None, :] * (2.0 * np.pi / SAMPLES)
    return np.stack([np.cos(angle), np.sin(angle)], axis=1).astype(np.float32)


def combine(terms):
    total = None
    for gain, value in terms:
        if abs(gain) < 1e-9:
            continue
        if abs(abs(gain) - 1.0) < 1e-9:
            if total is None:
                total = value if gain > 0 else -value
            else:
                total = total + value if gain > 0 else total - value
        else:
            scaled = value * np.float32(gain)
            total = scaled if total is None else total + scaled
    return total


def cosine(k):
    return math.cos(2.0 * math.pi * k / 16)


def sine(k):
    return math.sin(2.0 * math.pi * k / 16)


def forward16(a):
    s = [a[j] + a[j + 8] for j in range(8)]
    d = [a[j] - a[j + 8] for j in range(8)]
    out = [None] * 9
    p = [None] + [d[j] - d[8 - j] for j in range(1, 4)]
    q = [None] + [d[j] + d[8 - j] for j in range(1, 4)]
    for f in (1, 3, 5, 7):
        real = combine([(1.0, d[0])] + [(cosine(j * f), p[j]) for j in range(1, 4)])
        imag = combine([(-sine(4 * f), d[4])] + [(-sine(j * f), q[j]) for j in range(1, 4)])
        out[f] = (real, imag)
    s2 = [s[j] + s[j + 4] for j in range(4)]
    d2 = [s[j] - s[j + 4] for j in range(4)]
    for f in (2, 6):
        real = combine([(1.0, d2[0]), (cosine(f), d2[1] - d2[3])])
        imag = combine([(-sine(2 * f), d2[2]), (-sine(f), d2[1] + d2[3])])
        out[f] = (real, imag)
    out[4] = (s2[0] - s2[2], s2[3] - s2[1])
    even, odd = s2[0] + s2[2], s2[1] + s2[3]
    out[0] = (even + odd, None)
    out[8] = (even - odd, None)
    return out


def inverse16(vr, vi):
    qr = [vr[0]] + [vr[f] + vr[16 - f] for f in range(1, 8)] + [vr[8]]
    qi = [None] + [vi[f] - vi[16 - f] for f in range(1, 8)]
    even, odd = [None] * 8, [None] * 8
    for t in range(5):
        ce = combine([(cosine(t * f), qr[f]) for f in (0, 2, 4, 6, 8)])
        se = combine([(sine(t * f), qi[f]) for f in (2, 4, 6)])
        co = combine([(cosine(t * f), qr[f]) for f in (1, 3, 5, 7)])
        so = combine([(sine(t * f), qi[f]) for f in (1, 3, 5, 7)])
        even[t] = ce if se is None else ce - se
        if co is None:
            odd[t] = -so
        else:
            odd[t] = co if so is None else co - so
        if 1 <= t <= 3:
            even[8 - t] = ce + se
            odd[8 - t] = -co - so
    return even, odd


def kernel(
    x_ref, pairs_ref, counts_ref, edges_ref, obs_hbm, tab_hbm, tabt_hbm, dft_hbm, idft_hbm, tw_hbm,
    adj_ref, mis_ref,
    tab, tabt, dft, idft, tw, obs, nf, z, reach, ab, xm, corr, wgt, own, psend, precv, v,
    field, fsend, frecv, ssend, srecv,
    load_sem, s_sem, r_sem, bs_sem, br_sem, x_ssem, x_rsem,
):
    blk = lax.axis_index("blk")
    band = lax.axis_index("band")
    n_blk = lax.axis_size("blk")

    def at(step):
        return (lax.rem(blk + step + n_blk, n_blk), band)

    partner = (blk, 1 - band)
    barrier = pltpu.get_barrier_semaphore()
    for where in (at(1), at(-1), at(2), at(-2), partner):
        pl.semaphore_signal(barrier, inc=1, device_id=where, device_id_type=MESH)

    loads = [
        pltpu.make_async_copy(src, dst, load_sem.at[i])
        for i, (src, dst) in enumerate(
            [(tw_hbm, tw), (dft_hbm, dft), (tab_hbm, tab), (obs_hbm, obs), (tabt_hbm, tabt), (idft_hbm, idft)]
        )
    ]
    for load in loads:
        load.start()

    values = x_ref[...].astype(jnp.float32)
    centred = values - jnp.mean(values, axis=1, keepdims=True)
    spread = jnp.sqrt(jnp.mean(centred * centred, axis=1, keepdims=True) + EPSILON)
    nf[...] = centred / spread

    chan_ids = lax.broadcasted_iota(jnp.int32, (128, PAIRS), 0)
    hits1 = (chan_ids == pairs_ref[0:1, :]).astype(jnp.float32)
    hits2 = (chan_ids == pairs_ref[1:2, :]).astype(jnp.float32)
    scatter = jnp.concatenate([hits1, hits2], axis=1).astype(jnp.bfloat16)[: 3 * CHAN]
    gather = jnp.concatenate([hits1.T, hits2.T], axis=0).astype(jnp.bfloat16)[:, : 3 * CHAN]

    loads[0].wait()
    for r in range(CHAN // 16):
        rows = slice(16 * r, 16 * r + 16)
        for h in range(N2 // 128):
            lanes = slice(128 * h, 128 * h + 128)
            a = [
                nf[rows, N2 * t + 128 * h : N2 * t + 128 * h + 128].astype(jnp.bfloat16).astype(jnp.float32)
                for t in range(N1)
            ]
            y = forward16(a)
            for f in range(N1):
                yr, yi = y[f] if f <= 8 else y[16 - f]
                c = tw[f, 0:1, lanes]
                s = tw[f, 1:2, lanes]
                if yi is None:
                    zr, zi = yr * c, -(yr * s)
                elif f <= 8:
                    zr, zi = yr * c + yi * s, yi * c - yr * s
                else:
                    zr, zi = yr * c - yi * s, -(yi * c) - yr * s
                z[32 * f + 16 * r : 32 * f + 16 * r + 16, lanes] = zr.astype(jnp.bfloat16)
                z[32 * f + 16 * r : 32 * f + 16 * r + 16, N2 + 128 * h : N2 + 128 * h + 128] = zi.astype(jnp.bfloat16)

    def spec_copy(g, hop):
        part = pl.ds(g * PER, PER)
        return pltpu.make_async_remote_copy(
            src_ref=reach.at[part, pl.ds(0, CHAN)],
            dst_ref=reach.at[part, pl.ds(CHAN * hop, CHAN)],
            send_sem=s_sem.at[hop - 1, g],
            recv_sem=r_sem.at[hop - 1, g],
            device_id=at(hop),
            device_id_type=MESH,
        )

    def grad_copy(g, hop):
        part = pl.ds(g * PER, PER)
        return pltpu.make_async_remote_copy(
            src_ref=psend.at[hop - 1, part],
            dst_ref=precv.at[hop - 1, part],
            send_sem=bs_sem.at[hop - 1, g],
            recv_sem=br_sem.at[hop - 1, g],
            device_id=at(-hop),
            device_id_type=MESH,
        )

    loads[1].wait()
    pl.semaphore_wait(barrier, 5)
    for g in range(CHUNKS):
        rows = PER * CHAN
        s = jnp.dot(z[rows * g : rows * (g + 1)], dft[...], preferred_element_type=jnp.float32)
        s = (s * (1.0 / math.sqrt(SAMPLES))).astype(jnp.bfloat16)
        reach[PER * g : PER * (g + 1), 0:CHAN, :] = s.reshape(PER, CHAN, 2 * F2)
        spec_copy(g, 1).start()
        spec_copy(g, 2).start()

    lane_bins = lax.broadcasted_iota(jnp.int32, (1, F2), 1) * N1

    def insides(f1):
        bins = lane_bins + f1
        return [(bins >= edges_ref[n]) & (bins < edges_ref[n + 1]) for n in range(BANDS)]

    loads[2].wait()
    corr[...] = jnp.zeros_like(corr)

    def correlate(g, carry):
        spec_copy(g, 1).wait_recv()
        spec_copy(g, 2).wait_recv()
        for i in range(PER):
            f1 = g * PER + i
            both = jnp.dot(gather, reach[f1], preferred_element_type=jnp.float32)
            ab[f1] = both.astype(jnp.bfloat16)
            ar, ai = both[:PAIRS, :F2], both[:PAIRS, F2:]
            br, bi = both[PAIRS:, :F2], both[PAIRS:, F2:]
            xr = ar * br + ai * bi
            xi = ai * br - ar * bi
            for n, inside in enumerate(insides(f1)):
                rows = slice(PAIRS * n, PAIRS * (n + 1))
                xm[rows, 2 * F2 * i : 2 * F2 * i + F2] = jnp.where(inside, xr, 0.0).astype(jnp.bfloat16)
                xm[rows, 2 * F2 * i + F2 : 2 * F2 * (i + 1)] = jnp.where(inside, xi, 0.0).astype(jnp.bfloat16)
        part = tab[pl.ds(g * PER, PER)].reshape(PER * 2 * F2, LAGS)
        corr[...] += jnp.dot(xm[...], part, preferred_element_type=jnp.float32)
        return carry

    lax.fori_loop(0, CHUNKS, correlate, 0)

    loads[3].wait()
    slot = lax.broadcasted_iota(jnp.int32, (PAIRS, 1), 0)
    live = (slot < counts_ref[0]).astype(jnp.float32)
    squares = jnp.zeros((PAIRS, 1), jnp.float32)
    for n in range(BANDS):
        rows = slice(PAIRS * n, PAIRS * (n + 1))
        residual = (corr[rows] - obs[n]) * live
        squares = squares + jnp.sum(residual * residual, axis=1, keepdims=True)
        wgt[rows] = (residual * (1.0 / math.sqrt(FREQ_BINS / 8.0))).astype(jnp.bfloat16)
    misfit = squares * (0.5 / (BANDS * LAGS))
    mis_ref[...] = jnp.broadcast_to(misfit, (PAIRS, PAIRS)).T[0:1]

    loads[4].wait()

    def spread_back(g, carry):
        for i in range(PER):
            f1 = g * PER + i
            raw = jnp.dot(wgt[...], tabt[f1], preferred_element_type=jnp.float32)
            ins = [jnp.concatenate([m, m], axis=1) for m in insides(f1)]
            grad = jnp.where(ins[0], raw[0:PAIRS], 0.0)
            grad = jnp.where(ins[1], raw[PAIRS : 2 * PAIRS], grad)
            grad = jnp.where(ins[2], raw[2 * PAIRS :], grad)
            gr, gi = grad[:, :F2], grad[:, F2:]
            both = ab[f1].astype(jnp.float32)
            ar, ai = both[:PAIRS, :F2], both[:PAIRS, F2:]
            br, bi = both[PAIRS:, :F2], both[PAIRS:, F2:]
            first = jnp.concatenate([gr * br - gi * bi, gr * bi + gi * br], axis=1)
            second = jnp.concatenate([gr * ar + gi * ai, gr * ai - gi * ar], axis=1)
            grads = jnp.concatenate([first, second], axis=0).astype(jnp.bfloat16)
            sums = jnp.dot(scatter, grads, preferred_element_type=jnp.float32)
            own[f1] = sums[:CHAN]
            psend[0, f1] = sums[CHAN : 2 * CHAN].astype(jnp.bfloat16)
            psend[1, f1] = sums[2 * CHAN :].astype(jnp.bfloat16)
        grad_copy(g, 1).start()
        grad_copy(g, 2).start()
        return carry

    lax.fori_loop(0, CHUNKS, spread_back, 0)

    loads[5].wait()

    def invert(g, carry):
        grad_copy(g, 1).wait_recv()
        grad_copy(g, 2).wait_recv()
        part = pl.ds(g * PER, PER)
        total = own[part] + precv[0, part].astype(jnp.float32) + precv[1, part].astype(jnp.float32)
        coeffs = total.astype(jnp.bfloat16).reshape(PER * CHAN, 2 * F2)
        u = jnp.dot(coeffs, idft[...], preferred_element_type=jnp.float32)
        for i in range(PER):
            f1 = g * PER + i
            ur, ui = u[CHAN * i : CHAN * (i + 1), :N2], u[CHAN * i : CHAN * (i + 1), N2:]
            c, s = tw[f1, 0:1], tw[f1, 1:2]
            v[f1, 0] = ur * c - ui * s
            v[f1, 1] = ur * s + ui * c
        return carry

    lax.fori_loop(0, CHUNKS, invert, 0)

    sign = (1 - 2 * band).astype(jnp.float32)
    half = N1 // 2 * N2
    for r in range(CHAN // 16):
        rows = slice(16 * r, 16 * r + 16)
        total_e = jnp.zeros((16, 128), jnp.float32)
        total_w = jnp.zeros((16, 128), jnp.float32)
        for h in range(N2 // 128):
            lanes = slice(128 * h, 128 * h + 128)
            vr = [v[f, 0, rows, lanes] for f in range(N1)]
            vi = [v[f, 1, rows, lanes] for f in range(N1)]
            even, odd = inverse16(vr, vi)
            for t in range(8):
                lo = N2 * t + 128 * h
                out = slice(lo, lo + 128)
                total_e = total_e + even[t]
                low, high = nf[rows, out], nf[rows, half + lo : half + lo + 128]
                total_w = total_w + (even[t] * (low + high) + odd[t] * (low - high))
                mine = odd[t] * sign
                field[rows, out] = even[t] + mine
                fsend[rows, out] = (even[t] - mine).astype(jnp.bfloat16)
        sum_u = jnp.sum(total_e, axis=1, keepdims=True) * (2.0 / SAMPLES)
        sum_w = jnp.sum(total_w, axis=1, keepdims=True) * (1.0 / SAMPLES)
        ssend[rows, 0:128] = jnp.broadcast_to(sum_u, (16, 128))
        ssend[rows, 128:256] = jnp.broadcast_to(sum_w, (16, 128))

    swaps = [
        pltpu.make_async_remote_copy(
            src_ref=src, dst_ref=dst, send_sem=x_ssem.at[i], recv_sem=x_rsem.at[i],
            device_id=partner, device_id_type=MESH,
        )
        for i, (src, dst) in enumerate([(ssend, srecv), (fsend, frecv)])
    ]
    for swap in swaps:
        swap.start()
    for swap in swaps:
        swap.wait()
    mean_u = ssend[:, 0:1] + srecv[:, 0:1]
    mean_w = ssend[:, 128:129] + srecv[:, 128:129]
    mine = nf[:, pl.ds(pl.multiple_of(band * half, half), half)]
    adj_ref[...] = (field[...] + frecv[...].astype(jnp.float32) - mean_u - mine * mean_w) / spread

    def drain(g, carry):
        for hop in (1, 2):
            spec_copy(g, hop).wait_send()
            grad_copy(g, hop).wait_send()
        return carry

    lax.fori_loop(0, CHUNKS, drain, 0)


def per_device(traces, pair_list, counts, band_edges, observed):
    bf16, f32 = jnp.bfloat16, jnp.float32
    table = lag_table()
    dft = dft_table()
    tables = [
        jnp.asarray(table),
        jnp.asarray(np.ascontiguousarray(np.swapaxes(table, 1, 2))),
        jnp.asarray(dft.astype(ml_dtypes.bfloat16)),
        jnp.asarray((dft.T / math.sqrt(SAMPLES)).astype(ml_dtypes.bfloat16)),
        jnp.asarray(twiddles()),
    ]
    vmem = pl.BlockSpec(memory_space=pltpu.VMEM)
    smem = pl.BlockSpec(memory_space=pltpu.SMEM)
    hbm = pl.BlockSpec(memory_space=pl.ANY)
    dma = pltpu.SemaphoreType.DMA
    adjoint, misfit = pl.pallas_call(
        kernel,
        out_shape=(
            jax.ShapeDtypeStruct((CHAN, SAMPLES // 2), f32),
            jax.ShapeDtypeStruct((1, PAIRS), f32),
        ),
        in_specs=[vmem, vmem, smem, smem] + [hbm] * 6,
        out_specs=(vmem, vmem),
        scratch_shapes=[
            pltpu.VMEM((N1, 2 * F2, LAGS), bf16),
            pltpu.VMEM((N1, LAGS, 2 * F2), bf16),
            pltpu.VMEM((2 * N2, 2 * F2), bf16),
            pltpu.VMEM((2 * F2, 2 * N2), bf16),
            pltpu.VMEM((N1, 2, N2), f32),
            pltpu.VMEM((BANDS, PAIRS, LAGS), f32),
            pltpu.VMEM((CHAN, SAMPLES), f32),
            pltpu.VMEM((N1 * CHAN, 2 * N2), bf16),
            pltpu.VMEM((N1, 3 * CHAN, 2 * F2), bf16),
            pltpu.VMEM((N1, 2 * PAIRS, 2 * F2), bf16),
            pltpu.VMEM((BANDS * PAIRS, PER * 2 * F2), bf16),
            pltpu.VMEM((BANDS * PAIRS, LAGS), f32),
            pltpu.VMEM((BANDS * PAIRS, LAGS), bf16),
            pltpu.VMEM((N1, CHAN, 2 * F2), f32),
            pltpu.VMEM((2, N1, CHAN, 2 * F2), bf16),
            pltpu.VMEM((2, N1, CHAN, 2 * F2), bf16),
            pltpu.VMEM((N1, 2, CHAN, N2), f32),
            pltpu.VMEM((CHAN, SAMPLES // 2), f32),
            pltpu.VMEM((CHAN, SAMPLES // 2), bf16),
            pltpu.VMEM((CHAN, SAMPLES // 2), bf16),
            pltpu.VMEM((CHAN, 256), f32),
            pltpu.VMEM((CHAN, 256), f32),
            dma((6,)),
            dma((2, CHUNKS)),
            dma((2, CHUNKS)),
            dma((2, CHUNKS)),
            dma((2, CHUNKS)),
            dma((2,)),
            dma((2,)),
        ],
        compiler_params=pltpu.CompilerParams(
            collective_id=0, has_side_effects=True, vmem_limit_bytes=48 << 20
        ),
        name="misfit_adjoint",
    )(traces, pair_list.T, counts, band_edges, jnp.transpose(observed, (1, 0, 2)), *tables)
    return adjoint, misfit.reshape(PAIRS)


def solution(mesh):
    in_specs = (
        P("blk", None),
        P(("blk", "band"), None),
        P(("blk", "band")),
        P(),
        P(("blk", "band"), None, None),
    )
    out_specs = (P("blk", "band"), P(("blk", "band")))
    return jax.shard_map(
        per_device, mesh=mesh, in_specs=in_specs, out_specs=out_specs, check_vma=False
    )
```

profile of v0, /device:TPU:0, one launch (start us, length us, event | category | flops | bytes accessed | tf_op | source)
XLA Modules:
  0.0 48.9 jit_solution(5732625679952350205)
XLA Ops:
  1.3 0.0 copy-start
  1.3 2.2 %copy-done = bf16[16,256,512]{2,1,0:T(8,128)(2,1)S(1)} copy-done((bf16[16,256,512]{2,1,0:T(8,128)(2,1)S(1)}, bf16[16,256,512]{2,1,0:T(8,128)(2,1)}, u32[]{:S(2)}) %copy-start) | copy-done | bytes 4194328
  3.5 0.0 copy-start.1
  3.5 1.1 %copy-done.1 = f32[128,3,512]{2,0,1:T(8,128)S(1)} copy-done((f32[128,3,512]{2,0,1:T(8,128)S(1)}, f32[128,3,512]{2,0,1:T(8,128)}, u32[]{:S(2)}) %copy-start.1) | copy-done | bytes 786456
  4.6 0.0 copy-start.2
  4.6 0.9 %copy-done.2 = bf16[32,4096]{1,0:T(8,128)(2,1)S(1)} copy-done((bf16[32,4096]{1,0:T(8,128)(2,1)S(1)}, bf16[32,4096]{1,0:T(8,128)(2,1)}, u32[]{:S(2)}) %copy-start.2) | copy-done | bytes 262168
  5.6 0.0 copy-start.3
  5.6 0.9 %copy-done.3 = bf16[256,512]{1,0:T(8,128)(2,1)S(1)} copy-done((bf16[256,512]{1,0:T(8,128)(2,1)S(1)}, bf16[256,512]{1,0:T(8,128)(2,1)}, u32[]{:S(2)}) %copy-start.3) | copy-done | bytes 262168
  6.5 0.0 copy-start.4
  6.5 0.9 %copy-done.4 = bf16[512,256]{1,0:T(8,128)(2,1)S(1)} copy-done((bf16[512,256]{1,0:T(8,128)(2,1)S(1)}, bf16[512,256]{1,0:T(8,128)(2,1)}, u32[]{:S(2)}) %copy-start.4) | copy-done | bytes 262168
  7.5 0.0 copy-start.5
  7.5 0.8 %copy-done.5 = f32[16,2,256]{2,1,0:T(2,128)S(1)} copy-done((f32[16,2,256]{2,1,0:T(2,128)S(1)}, f32[16,2,256]{2,1,0:T(2,128)}, u32[]{:S(2)}) %copy-start.5) | copy-done | bytes 32792
  8.2 0.0 copy-start.6
  8.2 0.7 %copy-done.6 = s32[128,2]{0,1:T(2,128)S(1)} copy-done((s32[128,2]{0,1:T(2,128)S(1)}, s32[128,2]{0,1:T(2,128)}, u32[]{:S(2)}) %copy-start.6) | copy-done | bytes 1048
  8.9 0.0 copy-start.7
  8.9 0.7 %copy-done.7 = s32[4]{0:T(128)S(1)} copy-done((s32[4]{0:T(128)S(1)}, s32[4]{0:T(128)}, u32[]{:S(2)}) %copy-start.7) | copy-done | bytes 40
  9.5 38.2 %misfit_adjoint.1 = (f32[32,2048]{1,0:T(8,128)S(1)}, f32[1,128]{1,0:T(1,128)S(1)}) custom-call(bf16[32,4096]{1,0:T(8,128)(2,1)S(1)} %copy-done.2, s32[2,128]{1,0:T(2,128)S(1)} %bitcast.4, s32[1]{0:T(128)S(6)} %copy.14.counts_ref, s32[4]{0:T(128)S(1)} %copy-done.7, f32[3,128,512]{2,1,0:T(8,128)S(1)} %bitcast.3, bf16[16,256,512]{2,1,0:T(8,128)(2,1)S(1)} %copy-done, ...), custom_call_target="tpu_custom_call" | custom-call | tf_op jit(solution)/shard_map/misfit_adjoint/pallas_call | solution.py:362
  47.7 0.7 %copy.15 = f32[32,2048]{1,0:T(8,128)} copy(f32[32,2048]{1,0:T(8,128)S(1)} %get-tuple-element.8) | data formatting | bytes 524288
  48.4 0.5 %copy.16 = f32[128]{0:T(128)} copy(f32[128]{0:T(128)S(1)} %bitcast.5) | data formatting | bytes 1024
Async XLA Ops:
  1.3 2.2 %copy-start = (bf16[16,256,512]{2,1,0:T(8,128)(2,1)S(1)}, bf16[16,256,512]{2,1,0:T(8,128)(2,1)}, u32[]{:S(2)}) copy-start(bf16[16,256,512]{2,1,0:T(8,128)(2,1)} %constant.10.clone.tab_hbm) | copy-start | bytes 12582916
  3.5 1.1 %copy-start.1 = (f32[128,3,512]{2,0,1:T(8,128)S(1)}, f32[128,3,512]{2,0,1:T(8,128)}, u32[]{:S(2)}) copy-start(f32[128,3,512]{2,0,1:T(8,128)} %param.14) | copy-start | bytes 2359300
  4.6 0.9 %copy-start.2 = (bf16[32,4096]{1,0:T(8,128)(2,1)S(1)}, bf16[32,4096]{1,0:T(8,128)(2,1)}, u32[]{:S(2)}) copy-start(bf16[32,4096]{1,0:T(8,128)(2,1)} %x_ref.1) | copy-start | bytes 786436
  5.6 0.9 %copy-start.3 = (bf16[256,512]{1,0:T(8,128)(2,1)S(1)}, bf16[256,512]{1,0:T(8,128)(2,1)}, u32[]{:S(2)}) copy-start(bf16[256,512]{1,0:T(8,128)(2,1)} %constant.13.clone.idft_hbm) | copy-start | bytes 786436
  6.5 0.9 %copy-start.4 = (bf16[512,256]{1,0:T(8,128)(2,1)S(1)}, bf16[512,256]{1,0:T(8,128)(2,1)}, u32[]{:S(2)}) copy-start(bf16[512,256]{1,0:T(8,128)(2,1)} %constant.12.clone.dft_hbm) | copy-start | bytes 786436
  7.5 0.8 %copy-start.5 = (f32[16,2,256]{2,1,0:T(2,128)S(1)}, f32[16,2,256]{2,1,0:T(2,128)}, u32[]{:S(2)}) copy-start(f32[16,2,256]{2,1,0:T(2,128)} %constant.14.clone.tw_hbm) | copy-start | bytes 98308
  8.2 0.7 %copy-start.6 = (s32[128,2]{0,1:T(2,128)S(1)}, s32[128,2]{0,1:T(2,128)}, u32[]{:S(2)}) copy-start(s32[128,2]{0,1:T(2,128)} %param.11) | copy-start | bytes 3076
  8.9 0.7 %copy-start.7 = (s32[4]{0:T(128)S(1)}, s32[4]{0:T(128)}, u32[]{:S(2)}) copy-start(s32[4]{0:T(128)} %edges_ref.1) | copy-start | bytes 52
where the time goes:
time: 49.3 us; the launch traced here: 48.9 us
  Pallas kernels  38.2 us (77%)
  local copies, waits for them, and re-layouts  9.47 us (19%)
  between operations  1.3 us (3%)
    pallas_call x1, Pallas kernels, per_device(): pl.pallas_call(kernel, out_shape=(jax.ShapeDtypeStruct((CHAN, SAMPLES //...  38.2 us
    unnamed x18, local copies, waits for them, and re-layouts  9.47 us

commit v1 on v0

--- a/solution.py
+++ b/solution.py
@@ -113,9 +113,9 @@
 
 
 def kernel(
-    x_ref, pairs_ref, counts_ref, edges_ref, obs_hbm, tab_hbm, tabt_hbm, dft_hbm, idft_hbm, tw_hbm,
+    x_hbm, pairs_hbm, counts_hbm, edges_hbm, obs_hbm, tab_hbm, tabt_hbm, dft_hbm, idft_hbm, tw_hbm,
     adj_ref, mis_ref,
-    tab, tabt, dft, idft, tw, obs, nf, z, reach, ab, xm, corr, wgt, own, psend, precv, v,
+    x_ref, pairs_ref, counts_ref, edges_ref, tab, tabt, dft, idft, tw, obs, nf, z, reach, ab, xm, corr, wgt, raw, own, psend, precv, v,
     field, fsend, frecv, ssend, srecv,
     load_sem, s_sem, r_sem, bs_sem, br_sem, x_ssem, x_rsem,
 ):
@@ -131,27 +131,33 @@
     for where in (at(1), at(-1), at(2), at(-2), partner):
         pl.semaphore_signal(barrier, inc=1, device_id=where, device_id_type=MESH)
 
-    loads = [
-        pltpu.make_async_copy(src, dst, load_sem.at[i])
-        for i, (src, dst) in enumerate(
-            [(tw_hbm, tw), (dft_hbm, dft), (tab_hbm, tab), (obs_hbm, obs), (tabt_hbm, tabt), (idft_hbm, idft)]
+    loads = {
+        name: pltpu.make_async_copy(src, dst, load_sem.at[i])
+        for i, (name, src, dst) in enumerate(
+            [
+                ("x", x_hbm, x_ref),
+                ("tw", tw_hbm, tw),
+                ("pairs", pairs_hbm, pairs_ref),
+                ("dft", dft_hbm, dft),
+                ("edges", edges_hbm, edges_ref),
+                ("counts", counts_hbm, counts_ref),
+                ("tab", tab_hbm, tab),
+                ("obs", obs_hbm, obs),
+                ("tabt", tabt_hbm, tabt),
+                ("idft", idft_hbm, idft),
+            ]
         )
-    ]
-    for load in loads:
+    }
+    for load in loads.values():
         load.start()
 
+    loads["x"].wait()
     values = x_ref[...].astype(jnp.float32)
     centred = values - jnp.mean(values, axis=1, keepdims=True)
     spread = jnp.sqrt(jnp.mean(centred * centred, axis=1, keepdims=True) + EPSILON)
     nf[...] = centred / spread
 
-    chan_ids = lax.broadcasted_iota(jnp.int32, (128, PAIRS), 0)
-    hits1 = (chan_ids == pairs_ref[0:1, :]).astype(jnp.float32)
-    hits2 = (chan_ids == pairs_ref[1:2, :]).astype(jnp.float32)
-    scatter = jnp.concatenate([hits1, hits2], axis=1).astype(jnp.bfloat16)[: 3 * CHAN]
-    gather = jnp.concatenate([hits1.T, hits2.T], axis=0).astype(jnp.bfloat16)[:, : 3 * CHAN]
-
-    loads[0].wait()
+    loads["tw"].wait()
     for r in range(CHAN // 16):
         rows = slice(16 * r, 16 * r + 16)
         for h in range(N2 // 128):
@@ -196,7 +202,7 @@
             device_id_type=MESH,
         )
 
-    loads[1].wait()
+    loads["dft"].wait()
     pl.semaphore_wait(barrier, 5)
     for g in range(CHUNKS):
         rows = PER * CHAN
@@ -206,13 +212,21 @@
         spec_copy(g, 1).start()
         spec_copy(g, 2).start()
 
+    loads["pairs"].wait()
+    chan_ids = lax.broadcasted_iota(jnp.int32, (128, PAIRS), 0)
+    hits1 = (chan_ids == pairs_ref[0:1, :]).astype(jnp.float32)
+    hits2 = (chan_ids == pairs_ref[1:2, :]).astype(jnp.float32)
+    scatter = jnp.concatenate([hits1, hits2], axis=1).astype(jnp.bfloat16)[: 3 * CHAN]
+    gather = jnp.concatenate([hits1.T, hits2.T], axis=0).astype(jnp.bfloat16)[:, : 3 * CHAN]
+
     lane_bins = lax.broadcasted_iota(jnp.int32, (1, F2), 1) * N1
 
     def insides(f1):
         bins = lane_bins + f1
         return [(bins >= edges_ref[n]) & (bins < edges_ref[n + 1]) for n in range(BANDS)]
 
-    loads[2].wait()
+    loads["edges"].wait()
+    loads["tab"].wait()
     corr[...] = jnp.zeros_like(corr)
 
     def correlate(g, carry):
@@ -236,7 +250,8 @@
 
     lax.fori_loop(0, CHUNKS, correlate, 0)
 
-    loads[3].wait()
+    loads["obs"].wait()
+    loads["counts"].wait()
     slot = lax.broadcasted_iota(jnp.int32, (PAIRS, 1), 0)
     live = (slot < counts_ref[0]).astype(jnp.float32)
     squares = jnp.zeros((PAIRS, 1), jnp.float32)
@@ -248,16 +263,17 @@
     misfit = squares * (0.5 / (BANDS * LAGS))
     mis_ref[...] = jnp.broadcast_to(misfit, (PAIRS, PAIRS)).T[0:1]
 
-    loads[4].wait()
+    loads["tabt"].wait()
 
     def spread_back(g, carry):
+        raw[...] = jnp.dot(wgt[...], tabt[g], preferred_element_type=jnp.float32)
         for i in range(PER):
             f1 = g * PER + i
-            raw = jnp.dot(wgt[...], tabt[f1], preferred_element_type=jnp.float32)
+            cols = slice(2 * F2 * i, 2 * F2 * (i + 1))
             ins = [jnp.concatenate([m, m], axis=1) for m in insides(f1)]
-            grad = jnp.where(ins[0], raw[0:PAIRS], 0.0)
-            grad = jnp.where(ins[1], raw[PAIRS : 2 * PAIRS], grad)
-            grad = jnp.where(ins[2], raw[2 * PAIRS :], grad)
+            grad = jnp.where(ins[0], raw[0:PAIRS, cols], 0.0)
+            grad = jnp.where(ins[1], raw[PAIRS : 2 * PAIRS, cols], grad)
+            grad = jnp.where(ins[2], raw[2 * PAIRS :, cols], grad)
             gr, gi = grad[:, :F2], grad[:, F2:]
             both = ab[f1].astype(jnp.float32)
             ar, ai = both[:PAIRS, :F2], both[:PAIRS, F2:]
@@ -275,7 +291,7 @@
 
     lax.fori_loop(0, CHUNKS, spread_back, 0)
 
-    loads[5].wait()
+    loads["idft"].wait()
 
     def invert(g, carry):
         grad_copy(g, 1).wait_recv()
@@ -350,14 +366,13 @@
     dft = dft_table()
     tables = [
         jnp.asarray(table),
-        jnp.asarray(np.ascontiguousarray(np.swapaxes(table, 1, 2))),
+        jnp.asarray(np.ascontiguousarray(np.swapaxes(table.reshape(CHUNKS, PER * 2 * F2, LAGS), 1, 2))),
         jnp.asarray(dft.astype(ml_dtypes.bfloat16)),
         jnp.asarray((dft.T / math.sqrt(SAMPLES)).astype(ml_dtypes.bfloat16)),
         jnp.asarray(twiddles()),
     ]
     vmem = pl.BlockSpec(memory_space=pltpu.VMEM)
-    smem = pl.BlockSpec(memory_space=pltpu.SMEM)
-    hbm = pl.BlockSpec(memory_space=pl.ANY)
+    hbm = pl.BlockSpec(memory_space=pltpu.HBM)
     dma = pltpu.SemaphoreType.DMA
     adjoint, misfit = pl.pallas_call(
         kernel,
@@ -365,11 +380,15 @@
             jax.ShapeDtypeStruct((CHAN, SAMPLES // 2), f32),
             jax.ShapeDtypeStruct((1, PAIRS), f32),
         ),
-        in_specs=[vmem, vmem, smem, smem] + [hbm] * 6,
+        in_specs=[hbm] * 10,
         out_specs=(vmem, vmem),
         scratch_shapes=[
+            pltpu.VMEM((CHAN, SAMPLES), bf16),
+            pltpu.VMEM((2, PAIRS), jnp.int32),
+            pltpu.SMEM((1,), jnp.int32),
+            pltpu.SMEM((BANDS + 1,), jnp.int32),
             pltpu.VMEM((N1, 2 * F2, LAGS), bf16),
-            pltpu.VMEM((N1, LAGS, 2 * F2), bf16),
+            pltpu.VMEM((CHUNKS, LAGS, PER * 2 * F2), bf16),
             pltpu.VMEM((2 * N2, 2 * F2), bf16),
             pltpu.VMEM((2 * F2, 2 * N2), bf16),
             pltpu.VMEM((N1, 2, N2), f32),
@@ -381,6 +400,7 @@
             pltpu.VMEM((BANDS * PAIRS, PER * 2 * F2), bf16),
             pltpu.VMEM((BANDS * PAIRS, LAGS), f32),
             pltpu.VMEM((BANDS * PAIRS, LAGS), bf16),
+            pltpu.VMEM((BANDS * PAIRS, PER * 2 * F2), f32),
             pltpu.VMEM((N1, CHAN, 2 * F2), f32),
             pltpu.VMEM((2, N1, CHAN, 2 * F2), bf16),
             pltpu.VMEM((2, N1, CHAN, 2 * F2), bf16),
@@ -390,7 +410,7 @@
             pltpu.VMEM((CHAN, SAMPLES // 2), bf16),
             pltpu.VMEM((CHAN, 256), f32),
             pltpu.VMEM((CHAN, 256), f32),
-            dma((6,)),
+            dma((10,)),
             dma((2, CHUNKS)),
             dma((2, CHUNKS)),
             dma((2, CHUNKS)),
@@ -399,7 +419,7 @@
             dma((2,)),
         ],
         compiler_params=pltpu.CompilerParams(
-            collective_id=0, has_side_effects=True, vmem_limit_bytes=48 << 20
+            collective_id=0, has_side_effects=True, vmem_limit_bytes=60 << 20
         ),
         name="misfit_adjoint",
     )(traces, pair_list.T, counts, band_edges, jnp.transpose(observed, (1, 0, 2)), *tables)

time: 49.3 us -> 41.9 us (0.85)
  the two profiles are of different devices: /device:TPU:0 before, /device:TPU:7 now
where the time goes in v1:
time: 41.9 us; the launch traced here: 41.1 us
  Pallas kernels  37 us (88%)
  local copies, waits for them, and re-layouts  2.8 us (7%)
  between operations  1.28 us (3%)
    pallas_call x1, Pallas kernels, per_device(): pl.pallas_call(kernel, out_shape=(jax.ShapeDtypeStruct((CHAN, SAMPLES //...  37 us
    unnamed x2, local copies, waits for them, and re-layouts  2.8 us

profile of v1, /device:TPU:7, one launch (start us, length us, event | category | flops | bytes accessed | tf_op | source)
XLA Modules:
  0.0 41.1 jit_solution(10223307465816874044)
XLA Ops:
  1.3 37.0 %misfit_adjoint.1 = (f32[32,2048]{1,0:T(8,128)}, f32[1,128]{1,0:T(1,128)}) custom-call(bf16[32,4096]{1,0:T(8,128)(2,1)} %x_hbm.1, s32[2,128]{1,0:T(2,128)} %bitcast.4, s32[1]{0:T(128)S(6)} %copy.14.counts_hbm, s32[4]{0:T(128)} %edges_hbm.1, f32[3,128,512]{2,1,0:T(8,128)} %bitcast.3, bf16[16,256,512]{2,1,0:T(8,128)(2,1)} %constant.10.clone.tab_hbm, ...), custom_call_target="tpu_custom_call" | custom-call | tf_op jit(solution)/shard_map/misfit_adjoint/pallas_call | solution.py:377
  38.3 1.7 %copy.15 = f32[32,2048]{1,0:T(8,128)} copy(f32[32,2048]{1,0:T(8,128)} %get-tuple-element.8) | data formatting | bytes 524288
  40.0 1.1 %copy.16 = f32[128]{0:T(128)} copy(f32[128]{0:T(128)} %bitcast.5) | data formatting | bytes 1024

commit v2 on v1

--- a/solution.py
+++ b/solution.py
@@ -115,9 +115,9 @@
 def kernel(
     x_hbm, pairs_hbm, counts_hbm, edges_hbm, obs_hbm, tab_hbm, tabt_hbm, dft_hbm, idft_hbm, tw_hbm,
     adj_ref, mis_ref,
-    x_ref, pairs_ref, counts_ref, edges_ref, tab, tabt, dft, idft, tw, obs, nf, z, reach, ab, xm, corr, wgt, raw, own, psend, precv, v,
-    field, fsend, frecv, ssend, srecv,
-    load_sem, s_sem, r_sem, bs_sem, br_sem, x_ssem, x_rsem,
+    x_ref, pairs_ref, counts_ref, edges_ref, tab, tabt, dft, idft, tw, obs, nf, z, reach, ab, xm, corr, wgt, raw, own, far, nsend, nrecv, fsend, frecv,
+    csend, crecv, v, field,
+    load_sem, fs_sem, fr_sem, ns_sem, nr_sem, bns_sem, bnr_sem, bfs_sem, bfr_sem, xs_sem, xr_sem,
 ):
     blk = lax.axis_index("blk")
     band = lax.axis_index("band")
@@ -126,9 +126,11 @@
     def at(step):
         return (lax.rem(blk + step + n_blk, n_blk), band)
 
+    odd = lax.rem(blk, 2)
+    mate = (blk + 1 - 2 * odd, band)
     partner = (blk, 1 - band)
     barrier = pltpu.get_barrier_semaphore()
-    for where in (at(1), at(-1), at(2), at(-2), partner):
+    for where in (at(2), at(-2), mate, partner):
         pl.semaphore_signal(barrier, inc=1, device_id=where, device_id_type=MESH)
 
     loads = {
@@ -155,7 +157,8 @@
     values = x_ref[...].astype(jnp.float32)
     centred = values - jnp.mean(values, axis=1, keepdims=True)
     spread = jnp.sqrt(jnp.mean(centred * centred, axis=1, keepdims=True) + EPSILON)
-    nf[...] = centred / spread
+    gain = 1.0 / spread
+    nf[...] = centred * gain
 
     loads["tw"].wait()
     for r in range(CHAN // 16):
@@ -180,37 +183,50 @@
                 z[32 * f + 16 * r : 32 * f + 16 * r + 16, lanes] = zr.astype(jnp.bfloat16)
                 z[32 * f + 16 * r : 32 * f + 16 * r + 16, N2 + 128 * h : N2 + 128 * h + 128] = zi.astype(jnp.bfloat16)
 
-    def spec_copy(g, hop):
-        part = pl.ds(g * PER, PER)
+    def remote(src, dst, sems, slot, where):
         return pltpu.make_async_remote_copy(
-            src_ref=reach.at[part, pl.ds(0, CHAN)],
-            dst_ref=reach.at[part, pl.ds(CHAN * hop, CHAN)],
-            send_sem=s_sem.at[hop - 1, g],
-            recv_sem=r_sem.at[hop - 1, g],
-            device_id=at(hop),
+            src_ref=src,
+            dst_ref=dst,
+            send_sem=sems[0].at[slot],
+            recv_sem=sems[1].at[slot],
+            device_id=where,
             device_id_type=MESH,
         )
 
-    def grad_copy(g, hop):
-        part = pl.ds(g * PER, PER)
-        return pltpu.make_async_remote_copy(
-            src_ref=psend.at[hop - 1, part],
-            dst_ref=precv.at[hop - 1, part],
-            send_sem=bs_sem.at[hop - 1, g],
-            recv_sem=br_sem.at[hop - 1, g],
-            device_id=at(-hop),
-            device_id_type=MESH,
-        )
+    def chunk(g):
+        return pl.ds(g * PER, PER)
+
+    def far_spec(g):
+        src, dst = reach.at[chunk(g), pl.ds(0, CHAN)], reach.at[chunk(g), pl.ds(2 * CHAN, CHAN)]
+        return remote(src, dst, (fs_sem, fr_sem), g, at(2))
+
+    def near_spec(g):
+        lo = pl.multiple_of(odd * 2 * CHAN, CHAN)
+        src, dst = reach.at[chunk(g), pl.ds(lo, CHAN)], reach.at[chunk(g), pl.ds(CHAN, CHAN)]
+        return remote(src, dst, (ns_sem, nr_sem), g, mate)
+
+    def near_grad(g):
+        return remote(nsend.at[chunk(g)], nrecv.at[chunk(g)], (bns_sem, bnr_sem), g, mate)
+
+    def far_grad(g):
+        return remote(fsend.at[chunk(g)], frecv.at[chunk(g)], (bfs_sem, bfr_sem), g, at(-2))
+
+    def swap(g):
+        return remote(csend.at[chunk(g)], crecv.at[chunk(g)], (xs_sem, xr_sem), g, partner)
 
     loads["dft"].wait()
-    pl.semaphore_wait(barrier, 5)
+    pl.semaphore_wait(barrier, 4)
     for g in range(CHUNKS):
         rows = PER * CHAN
         s = jnp.dot(z[rows * g : rows * (g + 1)], dft[...], preferred_element_type=jnp.float32)
         s = (s * (1.0 / math.sqrt(SAMPLES))).astype(jnp.bfloat16)
         reach[PER * g : PER * (g + 1), 0:CHAN, :] = s.reshape(PER, CHAN, 2 * F2)
-        spec_copy(g, 1).start()
-        spec_copy(g, 2).start()
+        far_spec(g).start()
+
+        @pl.when(odd == 0)
+        def _():
+            near_spec(g).start()
+
 
     loads["pairs"].wait()
     chan_ids = lax.broadcasted_iota(jnp.int32, (128, PAIRS), 0)
@@ -230,8 +246,13 @@
     corr[...] = jnp.zeros_like(corr)
 
     def correlate(g, carry):
-        spec_copy(g, 1).wait_recv()
-        spec_copy(g, 2).wait_recv()
+        far_spec(g).wait_recv()
+
+        @pl.when(odd == 1)
+        def _():
+            near_spec(g).start()
+
+        near_spec(g).wait_recv()
         for i in range(PER):
             f1 = g * PER + i
             both = jnp.dot(gather, reach[f1], preferred_element_type=jnp.float32)
@@ -283,21 +304,53 @@
             grads = jnp.concatenate([first, second], axis=0).astype(jnp.bfloat16)
             sums = jnp.dot(scatter, grads, preferred_element_type=jnp.float32)
             own[f1] = sums[:CHAN]
-            psend[0, f1] = sums[CHAN : 2 * CHAN].astype(jnp.bfloat16)
-            psend[1, f1] = sums[2 * CHAN :].astype(jnp.bfloat16)
-        grad_copy(g, 1).start()
-        grad_copy(g, 2).start()
+            nsend[f1] = sums[CHAN : 2 * CHAN].astype(jnp.bfloat16)
+            far[f1] = sums[2 * CHAN :]
+        near_grad(g).start()
+
+        @pl.when(odd == 0)
+        def _():
+            fsend[chunk(g)] = far[chunk(g)].astype(jnp.bfloat16)
+            far_grad(g).start()
+
+        @pl.when((odd == 1) & (g > 0))
+        def _():
+            pass_on(g - 1)
+
         return carry
 
+    def pass_on(g):
+        near_grad(g).wait_recv()
+        fsend[chunk(g)] = (far[chunk(g)] + nrecv[chunk(g)].astype(jnp.float32)).astype(jnp.bfloat16)
+        far_grad(g).start()
+
     lax.fori_loop(0, CHUNKS, spread_back, 0)
 
+    @pl.when(odd == 1)
+    def _():
+        pass_on(CHUNKS - 1)
+
+    def gather_sums(g, carry):
+        far_grad(g).wait_recv()
+        total = own[chunk(g)] + frecv[chunk(g)].astype(jnp.float32)
+        own[chunk(g)] = total
+
+        @pl.when(odd == 0)
+        def _():
+            near_grad(g).wait_recv()
+            own[chunk(g)] += nrecv[chunk(g)].astype(jnp.float32)
+
+        csend[chunk(g)] = own[chunk(g)].astype(jnp.bfloat16)
+        swap(g).start()
+        return carry
+
+    lax.fori_loop(0, CHUNKS, gather_sums, 0)
+
     loads["idft"].wait()
 
     def invert(g, carry):
-        grad_copy(g, 1).wait_recv()
-        grad_copy(g, 2).wait_recv()
-        part = pl.ds(g * PER, PER)
-        total = own[part] + precv[0, part].astype(jnp.float32) + precv[1, part].astype(jnp.float32)
+        swap(g).wait_recv()
+        total = own[chunk(g)] + crecv[chunk(g)].astype(jnp.float32)
         coeffs = total.astype(jnp.bfloat16).reshape(PER * CHAN, 2 * F2)
         u = jnp.dot(coeffs, idft[...], preferred_element_type=jnp.float32)
         for i in range(PER):
@@ -320,41 +373,22 @@
             lanes = slice(128 * h, 128 * h + 128)
             vr = [v[f, 0, rows, lanes] for f in range(N1)]
             vi = [v[f, 1, rows, lanes] for f in range(N1)]
-            even, odd = inverse16(vr, vi)
+            even, odds = inverse16(vr, vi)
             for t in range(8):
                 lo = N2 * t + 128 * h
                 out = slice(lo, lo + 128)
                 total_e = total_e + even[t]
                 low, high = nf[rows, out], nf[rows, half + lo : half + lo + 128]
-                total_w = total_w + (even[t] * (low + high) + odd[t] * (low - high))
-                mine = odd[t] * sign
-                field[rows, out] = even[t] + mine
-                fsend[rows, out] = (even[t] - mine).astype(jnp.bfloat16)
-        sum_u = jnp.sum(total_e, axis=1, keepdims=True) * (2.0 / SAMPLES)
-        sum_w = jnp.sum(total_w, axis=1, keepdims=True) * (1.0 / SAMPLES)
-        ssend[rows, 0:128] = jnp.broadcast_to(sum_u, (16, 128))
-        ssend[rows, 128:256] = jnp.broadcast_to(sum_w, (16, 128))
-
-    swaps = [
-        pltpu.make_async_remote_copy(
-            src_ref=src, dst_ref=dst, send_sem=x_ssem.at[i], recv_sem=x_rsem.at[i],
-            device_id=partner, device_id_type=MESH,
-        )
-        for i, (src, dst) in enumerate([(ssend, srecv), (fsend, frecv)])
-    ]
-    for swap in swaps:
-        swap.start()
-    for swap in swaps:
-        swap.wait()
-    mean_u = ssend[:, 0:1] + srecv[:, 0:1]
-    mean_w = ssend[:, 128:129] + srecv[:, 128:129]
-    mine = nf[:, pl.ds(pl.multiple_of(band * half, half), half)]
-    adj_ref[...] = (field[...] + frecv[...].astype(jnp.float32) - mean_u - mine * mean_w) / spread
+                total_w = total_w + (even[t] * (low + high) + odds[t] * (low - high))
+                field[rows, out] = even[t] + odds[t] * sign
+        mean_u = jnp.sum(total_e, axis=1, keepdims=True) * (2.0 / SAMPLES)
+        mean_w = jnp.sum(total_w, axis=1, keepdims=True) * (1.0 / SAMPLES)
+        mine = nf[rows, pl.ds(pl.multiple_of(band * half, half), half)]
+        adj_ref[rows] = (field[rows] - mean_u - mine * mean_w) * gain[rows]
 
     def drain(g, carry):
-        for hop in (1, 2):
-            spec_copy(g, hop).wait_send()
-            grad_copy(g, hop).wait_send()
+        for copy in (far_spec, near_spec, near_grad, far_grad, swap):
+            copy(g).wait_send()
         return carry
 
     lax.fori_loop(0, CHUNKS, drain, 0)
@@ -377,8 +411,8 @@
     adjoint, misfit = pl.pallas_call(
         kernel,
         out_shape=(
-            jax.ShapeDtypeStruct((CHAN, SAMPLES // 2), f32),
-            jax.ShapeDtypeStruct((1, PAIRS), f32),
+            pltpu.VMEM((CHAN, SAMPLES // 2), f32),
+            pltpu.VMEM((1, PAIRS), f32),
         ),
         in_specs=[hbm] * 10,
         out_specs=(vmem, vmem),
@@ -402,21 +436,12 @@
             pltpu.VMEM((BANDS * PAIRS, LAGS), bf16),
             pltpu.VMEM((BANDS * PAIRS, PER * 2 * F2), f32),
             pltpu.VMEM((N1, CHAN, 2 * F2), f32),
-            pltpu.VMEM((2, N1, CHAN, 2 * F2), bf16),
-            pltpu.VMEM((2, N1, CHAN, 2 * F2), bf16),
+            pltpu.VMEM((N1, CHAN, 2 * F2), f32),
+            *[pltpu.VMEM((N1, CHAN, 2 * F2), bf16)] * 6,
             pltpu.VMEM((N1, 2, CHAN, N2), f32),
             pltpu.VMEM((CHAN, SAMPLES // 2), f32),
-            pltpu.VMEM((CHAN, SAMPLES // 2), bf16),
-            pltpu.VMEM((CHAN, SAMPLES // 2), bf16),
-            pltpu.VMEM((CHAN, 256), f32),
-            pltpu.VMEM((CHAN, 256), f32),
             dma((10,)),
-            dma((2, CHUNKS)),
-            dma((2, CHUNKS)),
-            dma((2, CHUNKS)),
-            dma((2, CHUNKS)),
-            dma((2,)),
-            dma((2,)),
+            *[dma((CHUNKS,))] * 10,
         ],
         compiler_params=pltpu.CompilerParams(
             collective_id=0, has_side_effects=True, vmem_limit_bytes=60 << 20

time: 41.9 us -> 36.4 us (0.87); the launches traced: 41.1 us -> 36.3 us
  Pallas kernels: 37 us -> 33.8 us
  local copies, waits for them, and re-layouts: 2.8 us -> 1.22 us
    pallas_call x1, Pallas kernels: 37 us -> 33.8 us  [per_device(): pl.pallas_call(kernel, out_shape=(pltpu.VMEM((CHAN, SAMPLES // 2), f32),...]
    unnamed x2, local copies, waits for them, and re-layouts: 2.8 us -> 1.22 us
where the time goes in v2:
time: 36.4 us; the launch traced here: 36.3 us
  Pallas kernels  33.8 us (93%)
  between operations  1.28 us (4%)
  local copies, waits for them, and re-layouts  1.22 us (3%)
    pallas_call x1, Pallas kernels, per_device(): pl.pallas_call(kernel, out_shape=(pltpu.VMEM((CHAN, SAMPLES // 2), f32),...  33.8 us
    unnamed x2, local copies, waits for them, and re-layouts  1.22 us

profile of v2, /device:TPU:7, one launch (start us, length us, event | category | flops | bytes accessed | tf_op | source)
XLA Modules:
  0.0 36.3 jit_solution(8786612548496060398)
XLA Ops:
  1.3 33.8 %misfit_adjoint.1 = (f32[32,2048]{1,0:T(8,128)S(1)}, f32[1,128]{1,0:T(1,128)S(1)}) custom-call(bf16[32,4096]{1,0:T(8,128)(2,1)} %x_hbm.1, s32[2,128]{1,0:T(2,128)} %bitcast.5, s32[1]{0:T(128)S(6)} %copy.16.counts_hbm, s32[4]{0:T(128)} %edges_hbm.1, f32[3,128,512]{2,1,0:T(8,128)} %bitcast.4, bf16[16,256,512]{2,1,0:T(8,128)(2,1)} %constant.10.clone.tab_hbm, ...), custom_call_target="tpu_custom_call" | custom-call | tf_op jit(solution)/shard_map/misfit_adjoint/pallas_call | solution.py:411
  35.1 0.7 %copy.14 = f32[32,2048]{1,0:T(8,128)} copy(f32[32,2048]{1,0:T(8,128)S(1)} %get-tuple-element.6) | data formatting | bytes 524288
  35.8 0.5 %copy.15 = f32[128]{0:T(128)} copy(f32[128]{0:T(128)S(1)} %bitcast.3) | data formatting | bytes 1024

commit v3 on v2

--- a/solution.py
+++ b/solution.py
@@ -21,8 +21,9 @@
 N1 = 16
 N2 = 256
 F2 = FREQ_BINS // N1
-CHUNKS = 4
-PER = N1 // CHUNKS
+PARTS = ((0, 2), (2, 6), (6, 10), (10, 14), (14, 16))
+CHUNKS = len(PARTS)
+WIDEST = 4
 MESH = pl.DeviceIdType.MESH
 
 
@@ -115,9 +116,9 @@
 def kernel(
     x_hbm, pairs_hbm, counts_hbm, edges_hbm, obs_hbm, tab_hbm, tabt_hbm, dft_hbm, idft_hbm, tw_hbm,
     adj_ref, mis_ref,
-    x_ref, pairs_ref, counts_ref, edges_ref, tab, tabt, dft, idft, tw, obs, nf, z, reach, ab, xm, corr, wgt, raw, own, far, nsend, nrecv, fsend, frecv,
-    csend, crecv, v, field,
-    load_sem, fs_sem, fr_sem, ns_sem, nr_sem, bns_sem, bnr_sem, bfs_sem, bfr_sem, xs_sem, xr_sem,
+    x_ref, pairs_ref, counts_ref, edges_ref, tab, tabt, dft, idft, tw, obs, nf, z, reach, ab, xm, corr, wgt, raw0, raw1, own, far, nsend, nrecv, fsend, frecv,
+    csend, crecv, ssend, srecv, v, field,
+    load_sem, fs_sem, fr_sem, ns_sem, nr_sem, bns_sem, bnr_sem, bfs_sem, bfr_sem, xs_sem, xr_sem, ms_sem, mr_sem,
 ):
     blk = lax.axis_index("blk")
     band = lax.axis_index("band")
@@ -130,7 +131,7 @@
     mate = (blk + 1 - 2 * odd, band)
     partner = (blk, 1 - band)
     barrier = pltpu.get_barrier_semaphore()
-    for where in (at(2), at(-2), mate, partner):
+    for where in (at(-2), mate, partner):
         pl.semaphore_signal(barrier, inc=1, device_id=where, device_id_type=MESH)
 
     loads = {
@@ -194,7 +195,8 @@
         )
 
     def chunk(g):
-        return pl.ds(g * PER, PER)
+        lo, hi = PARTS[g]
+        return pl.ds(lo, hi - lo)
 
     def far_spec(g):
         src, dst = reach.at[chunk(g), pl.ds(0, CHAN)], reach.at[chunk(g), pl.ds(2 * CHAN, CHAN)]
@@ -211,16 +213,20 @@
     def far_grad(g):
         return remote(fsend.at[chunk(g)], frecv.at[chunk(g)], (bfs_sem, bfr_sem), g, at(-2))
 
-    def swap(g):
-        return remote(csend.at[chunk(g)], crecv.at[chunk(g)], (xs_sem, xr_sem), g, partner)
+    def swap(r):
+        rows = pl.ds(16 * r, 16)
+        return remote(csend.at[rows], crecv.at[rows], (xs_sem, xr_sem), r, partner)
+
+    def swap_means(r):
+        rows = pl.ds(16 * r, 16)
+        return remote(ssend.at[rows], srecv.at[rows], (ms_sem, mr_sem), r, partner)
 
     loads["dft"].wait()
-    pl.semaphore_wait(barrier, 4)
-    for g in range(CHUNKS):
-        rows = PER * CHAN
-        s = jnp.dot(z[rows * g : rows * (g + 1)], dft[...], preferred_element_type=jnp.float32)
+    pl.semaphore_wait(barrier, 3)
+    for g, (lo, hi) in enumerate(PARTS):
+        s = jnp.dot(z[CHAN * lo : CHAN * hi], dft[...], preferred_element_type=jnp.float32)
         s = (s * (1.0 / math.sqrt(SAMPLES))).astype(jnp.bfloat16)
-        reach[PER * g : PER * (g + 1), 0:CHAN, :] = s.reshape(PER, CHAN, 2 * F2)
+        reach[lo:hi, 0:CHAN, :] = s.reshape(hi - lo, CHAN, 2 * F2)
         far_spec(g).start()
 
         @pl.when(odd == 0)
@@ -243,33 +249,33 @@
 
     loads["edges"].wait()
     loads["tab"].wait()
-    corr[...] = jnp.zeros_like(corr)
-
-    def correlate(g, carry):
+    for g, (lo, hi) in enumerate(PARTS):
         far_spec(g).wait_recv()
 
         @pl.when(odd == 1)
-        def _():
+        def _(g=g):
             near_spec(g).start()
 
         near_spec(g).wait_recv()
-        for i in range(PER):
-            f1 = g * PER + i
+        for f1 in range(lo, hi):
             both = jnp.dot(gather, reach[f1], preferred_element_type=jnp.float32)
-            ab[f1] = both.astype(jnp.bfloat16)
+            ab[f1] = both
             ar, ai = both[:PAIRS, :F2], both[:PAIRS, F2:]
             br, bi = both[PAIRS:, :F2], both[PAIRS:, F2:]
             xr = ar * br + ai * bi
             xi = ai * br - ar * bi
+            col = 2 * F2 * (f1 - lo)
             for n, inside in enumerate(insides(f1)):
                 rows = slice(PAIRS * n, PAIRS * (n + 1))
-                xm[rows, 2 * F2 * i : 2 * F2 * i + F2] = jnp.where(inside, xr, 0.0).astype(jnp.bfloat16)
-                xm[rows, 2 * F2 * i + F2 : 2 * F2 * (i + 1)] = jnp.where(inside, xi, 0.0).astype(jnp.bfloat16)
-        part = tab[pl.ds(g * PER, PER)].reshape(PER * 2 * F2, LAGS)
-        corr[...] += jnp.dot(xm[...], part, preferred_element_type=jnp.float32)
-        return carry
-
-    lax.fori_loop(0, CHUNKS, correlate, 0)
+                xm[rows, col : col + F2] = jnp.where(inside, xr, 0.0).astype(jnp.bfloat16)
+                xm[rows, col + F2 : col + 2 * F2] = jnp.where(inside, xi, 0.0).astype(jnp.bfloat16)
+        width = 2 * F2 * (hi - lo)
+        part = tab[lo:hi].reshape(width, LAGS)
+        term = jnp.dot(xm[:, :width], part, preferred_element_type=jnp.float32)
+        if g == 0:
+            corr[...] = term
+        else:
+            corr[...] += term
 
     loads["obs"].wait()
     loads["counts"].wait()
@@ -286,19 +292,31 @@
 
     loads["tabt"].wait()
 
-    def spread_back(g, carry):
-        raw[...] = jnp.dot(wgt[...], tabt[g], preferred_element_type=jnp.float32)
-        for i in range(PER):
-            f1 = g * PER + i
-            cols = slice(2 * F2 * i, 2 * F2 * (i + 1))
+    def lag_adjoint(g):
+        lo, hi = PARTS[g]
+        cols = slice(2 * F2 * lo, 2 * F2 * hi)
+        out = (raw0, raw1)[g % 2]
+        out[:, : 2 * F2 * (hi - lo)] = jnp.dot(wgt[...], tabt[:, cols], preferred_element_type=jnp.float32)
+
+    def pass_on(g):
+        near_grad(g).wait_recv()
+        fsend[chunk(g)] = (far[chunk(g)] + nrecv[chunk(g)].astype(jnp.float32)).astype(jnp.bfloat16)
+        far_grad(g).start()
+
+    lag_adjoint(0)
+    for g, (lo, hi) in enumerate(PARTS):
+        if g + 1 < CHUNKS:
+            lag_adjoint(g + 1)
+        raw = (raw0, raw1)[g % 2]
+        for f1 in range(lo, hi):
             ins = [jnp.concatenate([m, m], axis=1) for m in insides(f1)]
+            cols = slice(2 * F2 * (f1 - lo), 2 * F2 * (f1 - lo + 1))
             grad = jnp.where(ins[0], raw[0:PAIRS, cols], 0.0)
             grad = jnp.where(ins[1], raw[PAIRS : 2 * PAIRS, cols], grad)
             grad = jnp.where(ins[2], raw[2 * PAIRS :, cols], grad)
             gr, gi = grad[:, :F2], grad[:, F2:]
-            both = ab[f1].astype(jnp.float32)
-            ar, ai = both[:PAIRS, :F2], both[:PAIRS, F2:]
-            br, bi = both[PAIRS:, :F2], both[PAIRS:, F2:]
+            ar, ai = ab[f1, :PAIRS, :F2], ab[f1, :PAIRS, F2:]
+            br, bi = ab[f1, PAIRS:, :F2], ab[f1, PAIRS:, F2:]
             first = jnp.concatenate([gr * br - gi * bi, gr * bi + gi * br], axis=1)
             second = jnp.concatenate([gr * ar + gi * ai, gr * ai - gi * ar], axis=1)
             grads = jnp.concatenate([first, second], axis=0).astype(jnp.bfloat16)
@@ -309,59 +327,38 @@
         near_grad(g).start()
 
         @pl.when(odd == 0)
-        def _():
+        def _(g=g):
             fsend[chunk(g)] = far[chunk(g)].astype(jnp.bfloat16)
             far_grad(g).start()
 
-        @pl.when((odd == 1) & (g > 0))
-        def _():
-            pass_on(g - 1)
-
-        return carry
-
-    def pass_on(g):
-        near_grad(g).wait_recv()
-        fsend[chunk(g)] = (far[chunk(g)] + nrecv[chunk(g)].astype(jnp.float32)).astype(jnp.bfloat16)
-        far_grad(g).start()
-
-    lax.fori_loop(0, CHUNKS, spread_back, 0)
+        if g > 0:
+
+            @pl.when(odd == 1)
+            def _(g=g):
+                pass_on(g - 1)
 
     @pl.when(odd == 1)
     def _():
         pass_on(CHUNKS - 1)
 
-    def gather_sums(g, carry):
+    loads["idft"].wait()
+    for g, (lo, hi) in enumerate(PARTS):
         far_grad(g).wait_recv()
-        total = own[chunk(g)] + frecv[chunk(g)].astype(jnp.float32)
-        own[chunk(g)] = total
 
         @pl.when(odd == 0)
-        def _():
+        def _(g=g):
             near_grad(g).wait_recv()
             own[chunk(g)] += nrecv[chunk(g)].astype(jnp.float32)
 
-        csend[chunk(g)] = own[chunk(g)].astype(jnp.bfloat16)
-        swap(g).start()
-        return carry
-
-    lax.fori_loop(0, CHUNKS, gather_sums, 0)
-
-    loads["idft"].wait()
-
-    def invert(g, carry):
-        swap(g).wait_recv()
-        total = own[chunk(g)] + crecv[chunk(g)].astype(jnp.float32)
-        coeffs = total.astype(jnp.bfloat16).reshape(PER * CHAN, 2 * F2)
+        total = own[chunk(g)] + frecv[chunk(g)].astype(jnp.float32)
+        coeffs = total.astype(jnp.bfloat16).reshape((hi - lo) * CHAN, 2 * F2)
         u = jnp.dot(coeffs, idft[...], preferred_element_type=jnp.float32)
-        for i in range(PER):
-            f1 = g * PER + i
-            ur, ui = u[CHAN * i : CHAN * (i + 1), :N2], u[CHAN * i : CHAN * (i + 1), N2:]
+        for f1 in range(lo, hi):
+            rows = slice(CHAN * (f1 - lo), CHAN * (f1 - lo + 1))
+            ur, ui = u[rows, :N2], u[rows, N2:]
             c, s = tw[f1, 0:1], tw[f1, 1:2]
             v[f1, 0] = ur * c - ui * s
             v[f1, 1] = ur * s + ui * c
-        return carry
-
-    lax.fori_loop(0, CHUNKS, invert, 0)
 
     sign = (1 - 2 * band).astype(jnp.float32)
     half = N1 // 2 * N2
@@ -380,18 +377,31 @@
                 total_e = total_e + even[t]
                 low, high = nf[rows, out], nf[rows, half + lo : half + lo + 128]
                 total_w = total_w + (even[t] * (low + high) + odds[t] * (low - high))
-                field[rows, out] = even[t] + odds[t] * sign
+                mine = odds[t] * sign
+                field[rows, out] = even[t] + mine
+                csend[rows, out] = (even[t] - mine).astype(jnp.bfloat16)
         mean_u = jnp.sum(total_e, axis=1, keepdims=True) * (2.0 / SAMPLES)
         mean_w = jnp.sum(total_w, axis=1, keepdims=True) * (1.0 / SAMPLES)
+        lane = lax.broadcasted_iota(jnp.int32, (16, 128), 1)
+        ssend[rows] = jnp.where(lane == 0, mean_u, mean_w)
+        swap_means(r).start()
+        swap(r).start()
+
+    for r in range(CHAN // 16):
+        rows = slice(16 * r, 16 * r + 16)
+        swap_means(r).wait_recv()
+        means = ssend[rows] + srecv[rows]
         mine = nf[rows, pl.ds(pl.multiple_of(band * half, half), half)]
-        adj_ref[rows] = (field[rows] - mean_u - mine * mean_w) * gain[rows]
-
-    def drain(g, carry):
-        for copy in (far_spec, near_spec, near_grad, far_grad, swap):
+        partial = field[rows] - means[:, 0:1] - mine * means[:, 1:2]
+        swap(r).wait_recv()
+        adj_ref[rows] = (partial + crecv[rows].astype(jnp.float32)) * gain[rows]
+
+    for g in range(CHUNKS):
+        for copy in (far_spec, near_spec, near_grad, far_grad):
             copy(g).wait_send()
-        return carry
-
-    lax.fori_loop(0, CHUNKS, drain, 0)
+    for r in range(CHAN // 16):
+        swap(r).wait_send()
+        swap_means(r).wait_send()
 
 
 def per_device(traces, pair_list, counts, band_edges, observed):
@@ -400,7 +410,7 @@
     dft = dft_table()
     tables = [
         jnp.asarray(table),
-        jnp.asarray(np.ascontiguousarray(np.swapaxes(table.reshape(CHUNKS, PER * 2 * F2, LAGS), 1, 2))),
+        jnp.asarray(np.ascontiguousarray(table.reshape(N1 * 2 * F2, LAGS).T)),
         jnp.asarray(dft.astype(ml_dtypes.bfloat16)),
         jnp.asarray((dft.T / math.sqrt(SAMPLES)).astype(ml_dtypes.bfloat16)),
         jnp.asarray(twiddles()),
@@ -422,7 +432,7 @@
             pltpu.SMEM((1,), jnp.int32),
             pltpu.SMEM((BANDS + 1,), jnp.int32),
             pltpu.VMEM((N1, 2 * F2, LAGS), bf16),
-            pltpu.VMEM((CHUNKS, LAGS, PER * 2 * F2), bf16),
+            pltpu.VMEM((LAGS, N1 * 2 * F2), bf16),
             pltpu.VMEM((2 * N2, 2 * F2), bf16),
             pltpu.VMEM((2 * F2, 2 * N2), bf16),
             pltpu.VMEM((N1, 2, N2), f32),
@@ -430,18 +440,22 @@
             pltpu.VMEM((CHAN, SAMPLES), f32),
             pltpu.VMEM((N1 * CHAN, 2 * N2), bf16),
             pltpu.VMEM((N1, 3 * CHAN, 2 * F2), bf16),
-            pltpu.VMEM((N1, 2 * PAIRS, 2 * F2), bf16),
-            pltpu.VMEM((BANDS * PAIRS, PER * 2 * F2), bf16),
+            pltpu.VMEM((N1, 2 * PAIRS, 2 * F2), f32),
+            pltpu.VMEM((BANDS * PAIRS, WIDEST * 2 * F2), bf16),
             pltpu.VMEM((BANDS * PAIRS, LAGS), f32),
             pltpu.VMEM((BANDS * PAIRS, LAGS), bf16),
-            pltpu.VMEM((BANDS * PAIRS, PER * 2 * F2), f32),
+            pltpu.VMEM((BANDS * PAIRS, WIDEST * 2 * F2), f32),
+            pltpu.VMEM((BANDS * PAIRS, WIDEST * 2 * F2), f32),
             pltpu.VMEM((N1, CHAN, 2 * F2), f32),
             pltpu.VMEM((N1, CHAN, 2 * F2), f32),
-            *[pltpu.VMEM((N1, CHAN, 2 * F2), bf16)] * 6,
+            *[pltpu.VMEM((N1, CHAN, 2 * F2), bf16)] * 4,
+            *[pltpu.VMEM((CHAN, SAMPLES // 2), bf16)] * 2,
+            *[pltpu.VMEM((CHAN, 128), f32)] * 2,
             pltpu.VMEM((N1, 2, CHAN, N2), f32),
             pltpu.VMEM((CHAN, SAMPLES // 2), f32),
             dma((10,)),
-            *[dma((CHUNKS,))] * 10,
+            *[dma((CHUNKS,))] * 8,
+            *[dma((CHAN // 16,))] * 4,
         ],
         compiler_params=pltpu.CompilerParams(
             collective_id=0, has_side_effects=True, vmem_limit_bytes=60 << 20

time: 36.4 us -> 34.1 us (0.937)
  Pallas kernels: 33.8 us -> 31.5 us
    pallas_call x1, Pallas kernels: 33.8 us -> 31.5 us  [per_device(): pl.pallas_call(kernel, out_shape=(pltpu.VMEM((CHAN, SAMPLES // 2), f32),...]
where the time goes in v3:
time: 34.1 us; the launch traced here: 34 us
  Pallas kernels  31.5 us (92%)
  between operations  1.28 us (4%)
  local copies, waits for them, and re-layouts  1.22 us (4%)
    pallas_call x1, Pallas kernels, per_device(): pl.pallas_call(kernel, out_shape=(pltpu.VMEM((CHAN, SAMPLES // 2), f32),...  31.5 us
    unnamed x2, local copies, waits for them, and re-layouts  1.22 us

profile of v3, /device:TPU:7, one launch (start us, length us, event | category | flops | bytes accessed | tf_op | source)
XLA Modules:
  0.0 34.0 jit_solution(17306915194172209159)
XLA Ops:
  1.3 31.5 %misfit_adjoint.1 = (f32[32,2048]{1,0:T(8,128)S(1)}, f32[1,128]{1,0:T(1,128)S(1)}) custom-call(bf16[32,4096]{1,0:T(8,128)(2,1)} %x_hbm.1, s32[2,128]{1,0:T(2,128)} %bitcast.5, s32[1]{0:T(128)S(6)} %copy.16.counts_hbm, s32[4]{0:T(128)} %edges_hbm.1, f32[3,128,512]{2,1,0:T(8,128)} %bitcast.4, bf16[16,256,512]{2,1,0:T(8,128)(2,1)} %constant.10.clone.tab_hbm, ...), custom_call_target="tpu_custom_call" | custom-call | tf_op jit(solution)/shard_map/misfit_adjoint/pallas_call | solution.py:421
  32.8 0.7 %copy.14 = f32[32,2048]{1,0:T(8,128)} copy(f32[32,2048]{1,0:T(8,128)S(1)} %get-tuple-element.6) | data formatting | bytes 524288
  33.5 0.5 %copy.15 = f32[128]{0:T(128)} copy(f32[128]{0:T(128)S(1)} %bitcast.3) | data formatting | bytes 1024

commit v4 on v3

--- a/solution.py
+++ b/solution.py
@@ -21,9 +21,10 @@
 N1 = 16
 N2 = 256
 F2 = FREQ_BINS // N1
-PARTS = ((0, 2), (2, 6), (6, 10), (10, 14), (14, 16))
+PARTS = ((0, 4), (4, 8), (8, 12), (12, 16))
 CHUNKS = len(PARTS)
 WIDEST = 4
+HALF = CHAN // 2
 MESH = pl.DeviceIdType.MESH
 
 
@@ -117,8 +118,8 @@
     x_hbm, pairs_hbm, counts_hbm, edges_hbm, obs_hbm, tab_hbm, tabt_hbm, dft_hbm, idft_hbm, tw_hbm,
     adj_ref, mis_ref,
     x_ref, pairs_ref, counts_ref, edges_ref, tab, tabt, dft, idft, tw, obs, nf, z, reach, ab, xm, corr, wgt, raw0, raw1, own, far, nsend, nrecv, fsend, frecv,
-    csend, crecv, ssend, srecv, v, field,
-    load_sem, fs_sem, fr_sem, ns_sem, nr_sem, bns_sem, bnr_sem, bfs_sem, bfr_sem, xs_sem, xr_sem, ms_sem, mr_sem,
+    csend, crecv, v, field,
+    load_sem, fs_sem, fr_sem, ns_sem, nr_sem, bns_sem, bnr_sem, bfs_sem, bfr_sem, xs_sem, xr_sem, lbs_sem, lbr_sem,
 ):
     blk = lax.axis_index("blk")
     band = lax.axis_index("band")
@@ -162,27 +163,31 @@
     nf[...] = centred * gain
 
     loads["tw"].wait()
-    for r in range(CHAN // 16):
-        rows = slice(16 * r, 16 * r + 16)
-        for h in range(N2 // 128):
-            lanes = slice(128 * h, 128 * h + 128)
-            a = [
-                nf[rows, N2 * t + 128 * h : N2 * t + 128 * h + 128].astype(jnp.bfloat16).astype(jnp.float32)
-                for t in range(N1)
-            ]
-            y = forward16(a)
-            for f in range(N1):
-                yr, yi = y[f] if f <= 8 else y[16 - f]
-                c = tw[f, 0:1, lanes]
-                s = tw[f, 1:2, lanes]
-                if yi is None:
-                    zr, zi = yr * c, -(yr * s)
-                elif f <= 8:
-                    zr, zi = yr * c + yi * s, yi * c - yr * s
-                else:
-                    zr, zi = yr * c - yi * s, -(yi * c) - yr * s
-                z[32 * f + 16 * r : 32 * f + 16 * r + 16, lanes] = zr.astype(jnp.bfloat16)
-                z[32 * f + 16 * r : 32 * f + 16 * r + 16, N2 + 128 * h : N2 + 128 * h + 128] = zi.astype(jnp.bfloat16)
+    def transform16(lo, hi):
+        for r in range(CHAN // 16):
+            rows = slice(16 * r, 16 * r + 16)
+            for h in range(N2 // 128):
+                lanes = slice(128 * h, 128 * h + 128)
+                a = [
+                    nf[rows, N2 * t + 128 * h : N2 * t + 128 * h + 128].astype(jnp.bfloat16).astype(jnp.float32)
+                    for t in range(N1)
+                ]
+                y = forward16(a)
+                for f in range(lo, hi):
+                    yr, yi = y[f] if f <= 8 else y[16 - f]
+                    c = tw[f, 0:1, lanes]
+                    s = tw[f, 1:2, lanes]
+                    if yi is None:
+                        zr, zi = yr * c, -(yr * s)
+                    elif f <= 8:
+                        zr, zi = yr * c + yi * s, yi * c - yr * s
+                    else:
+                        zr, zi = yr * c - yi * s, -(yi * c) - yr * s
+                    out = slice(32 * f + 16 * r, 32 * f + 16 * r + 16)
+                    z[out, lanes] = zr.astype(jnp.bfloat16)
+                    z[out, N2 + 128 * h : N2 + 128 * h + 128] = zi.astype(jnp.bfloat16)
+
+    transform16(*PARTS[0])
 
     def remote(src, dst, sems, slot, where):
         return pltpu.make_async_remote_copy(
@@ -210,20 +215,26 @@
     def near_grad(g):
         return remote(nsend.at[chunk(g)], nrecv.at[chunk(g)], (bns_sem, bnr_sem), g, mate)
 
+    def back(crosses):
+        return (at(-2)[0], jnp.where(crosses, 1 - band, band))
+
     def far_grad(g):
-        return remote(fsend.at[chunk(g)], frecv.at[chunk(g)], (bfs_sem, bfr_sem), g, at(-2))
+        rows = chunk(g), pl.ds(0, HALF)
+        return remote(fsend.at[rows], frecv.at[rows], (bfs_sem, bfr_sem), g, back(lax.rem(blk, 16) < 2))
+
+    def late_grad(i):
+        rows = pl.ds(i * N1 // 2, N1 // 2), pl.ds(HALF, HALF)
+        return remote(fsend.at[rows], frecv.at[rows], (lbs_sem, lbr_sem), i, at(-2))
 
     def swap(r):
         rows = pl.ds(16 * r, 16)
         return remote(csend.at[rows], crecv.at[rows], (xs_sem, xr_sem), r, partner)
 
-    def swap_means(r):
-        rows = pl.ds(16 * r, 16)
-        return remote(ssend.at[rows], srecv.at[rows], (ms_sem, mr_sem), r, partner)
-
     loads["dft"].wait()
     pl.semaphore_wait(barrier, 3)
     for g, (lo, hi) in enumerate(PARTS):
+        if g == 1:
+            transform16(lo, N1)
         s = jnp.dot(z[CHAN * lo : CHAN * hi], dft[...], preferred_element_type=jnp.float32)
         s = (s * (1.0 / math.sqrt(SAMPLES))).astype(jnp.bfloat16)
         reach[lo:hi, 0:CHAN, :] = s.reshape(hi - lo, CHAN, 2 * F2)
@@ -305,7 +316,7 @@
 
     lag_adjoint(0)
     for g, (lo, hi) in enumerate(PARTS):
-        if g + 1 < CHUNKS:
+        if 0 < g < CHUNKS - 1:
             lag_adjoint(g + 1)
         raw = (raw0, raw1)[g % 2]
         for f1 in range(lo, hi):
@@ -331,7 +342,9 @@
             fsend[chunk(g)] = far[chunk(g)].astype(jnp.bfloat16)
             far_grad(g).start()
 
-        if g > 0:
+        if g == 0:
+            lag_adjoint(1)
+        else:
 
             @pl.when(odd == 1)
             def _(g=g):
@@ -341,29 +354,42 @@
     def _():
         pass_on(CHUNKS - 1)
 
+    for i in range(2):
+        late_grad(i).start()
+
     loads["idft"].wait()
-    for g, (lo, hi) in enumerate(PARTS):
-        far_grad(g).wait_recv()
-
-        @pl.when(odd == 0)
-        def _(g=g):
+
+    @pl.when(odd == 0)
+    def _():
+        for g in range(CHUNKS):
             near_grad(g).wait_recv()
             own[chunk(g)] += nrecv[chunk(g)].astype(jnp.float32)
 
-        total = own[chunk(g)] + frecv[chunk(g)].astype(jnp.float32)
-        coeffs = total.astype(jnp.bfloat16).reshape((hi - lo) * CHAN, 2 * F2)
+    def invert(r, lo, hi):
+        rows = slice(HALF * r, HALF * (r + 1))
+        total = own[lo:hi, rows] + frecv[lo:hi, rows].astype(jnp.float32)
+        coeffs = total.astype(jnp.bfloat16).reshape((hi - lo) * HALF, 2 * F2)
         u = jnp.dot(coeffs, idft[...], preferred_element_type=jnp.float32)
         for f1 in range(lo, hi):
-            rows = slice(CHAN * (f1 - lo), CHAN * (f1 - lo + 1))
-            ur, ui = u[rows, :N2], u[rows, N2:]
+            part = slice(HALF * (f1 - lo), HALF * (f1 - lo + 1))
+            ur, ui = u[part, :N2], u[part, N2:]
             c, s = tw[f1, 0:1], tw[f1, 1:2]
-            v[f1, 0] = ur * c - ui * s
-            v[f1, 1] = ur * s + ui * c
+            v[f1, 0, rows] = ur * c - ui * s
+            v[f1, 1, rows] = ur * s + ui * c
 
     sign = (1 - 2 * band).astype(jnp.float32)
     half = N1 // 2 * N2
+    my_means = []
     for r in range(CHAN // 16):
         rows = slice(16 * r, 16 * r + 16)
+        if r == 0:
+            for g in range(CHUNKS):
+                far_grad(g).wait_recv()
+                invert(0, *PARTS[g])
+        else:
+            for i in range(2):
+                late_grad(i).wait_recv()
+                invert(1, i * N1 // 2, (i + 1) * N1 // 2)
         total_e = jnp.zeros((16, 128), jnp.float32)
         total_w = jnp.zeros((16, 128), jnp.float32)
         for h in range(N2 // 128):
@@ -382,26 +408,31 @@
                 csend[rows, out] = (even[t] - mine).astype(jnp.bfloat16)
         mean_u = jnp.sum(total_e, axis=1, keepdims=True) * (2.0 / SAMPLES)
         mean_w = jnp.sum(total_w, axis=1, keepdims=True) * (1.0 / SAMPLES)
+        my_means.append((mean_u, mean_w))
         lane = lax.broadcasted_iota(jnp.int32, (16, 128), 1)
-        ssend[rows] = jnp.where(lane == 0, mean_u, mean_w)
-        swap_means(r).start()
+        high_u, high_w = mean_u.astype(jnp.bfloat16).astype(jnp.float32), mean_w.astype(jnp.bfloat16).astype(jnp.float32)
+        packed = jnp.where(lane == 0, high_u, jnp.where(lane == 1, mean_u - high_u, high_w))
+        packed = jnp.where(lane == 3, mean_w - high_w, packed)
+        csend[rows, half:] = packed.astype(jnp.bfloat16)
         swap(r).start()
 
     for r in range(CHAN // 16):
         rows = slice(16 * r, 16 * r + 16)
-        swap_means(r).wait_recv()
-        means = ssend[rows] + srecv[rows]
         mine = nf[rows, pl.ds(pl.multiple_of(band * half, half), half)]
-        partial = field[rows] - means[:, 0:1] - mine * means[:, 1:2]
         swap(r).wait_recv()
-        adj_ref[rows] = (partial + crecv[rows].astype(jnp.float32)) * gain[rows]
+        means = crecv[rows, half:].astype(jnp.float32)
+        mean_u = my_means[r][0] + (means[:, 0:1] + means[:, 1:2])
+        mean_w = my_means[r][1] + (means[:, 2:3] + means[:, 3:4])
+        total = field[rows] + crecv[rows, :half].astype(jnp.float32)
+        adj_ref[rows] = (total - mean_u - mine * mean_w) * gain[rows]
 
     for g in range(CHUNKS):
         for copy in (far_spec, near_spec, near_grad, far_grad):
             copy(g).wait_send()
+    for i in range(2):
+        late_grad(i).wait_send()
     for r in range(CHAN // 16):
         swap(r).wait_send()
-        swap_means(r).wait_send()
 
 
 def per_device(traces, pair_list, counts, band_edges, observed):
@@ -449,8 +480,7 @@
             pltpu.VMEM((N1, CHAN, 2 * F2), f32),
             pltpu.VMEM((N1, CHAN, 2 * F2), f32),
             *[pltpu.VMEM((N1, CHAN, 2 * F2), bf16)] * 4,
-            *[pltpu.VMEM((CHAN, SAMPLES // 2), bf16)] * 2,
-            *[pltpu.VMEM((CHAN, 128), f32)] * 2,
+            *[pltpu.VMEM((CHAN, SAMPLES // 2 + 128), bf16)] * 2,
             pltpu.VMEM((N1, 2, CHAN, N2), f32),
             pltpu.VMEM((CHAN, SAMPLES // 2), f32),
             dma((10,)),

time: 34.1 us -> 33.1 us (0.971)
  Pallas kernels: 31.5 us -> 30.5 us
    pallas_call x1, Pallas kernels: 31.5 us -> 30.5 us  [per_device(): pl.pallas_call(kernel, out_shape=(pltpu.VMEM((CHAN, SAMPLES // 2), f32),...]
where the time goes in v4:
time: 33.1 us; the launch traced here: 33 us
  Pallas kernels  30.5 us (92%)
  between operations  1.28 us (4%)
  local copies, waits for them, and re-layouts  1.22 us (4%)
    pallas_call x1, Pallas kernels, per_device(): pl.pallas_call(kernel, out_shape=(pltpu.VMEM((CHAN, SAMPLES // 2), f32),...  30.5 us
    unnamed x2, local copies, waits for them, and re-layouts  1.22 us

profile of v4, /device:TPU:7, one launch (start us, length us, event | category | flops | bytes accessed | tf_op | source)
XLA Modules:
  0.0 33.0 jit_solution(15615279346237246163)
XLA Ops:
  1.3 30.5 %misfit_adjoint.1 = (f32[32,2048]{1,0:T(8,128)S(1)}, f32[1,128]{1,0:T(1,128)S(1)}) custom-call(bf16[32,4096]{1,0:T(8,128)(2,1)} %x_hbm.1, s32[2,128]{1,0:T(2,128)} %bitcast.5, s32[1]{0:T(128)S(6)} %copy.16.counts_hbm, s32[4]{0:T(128)} %edges_hbm.1, f32[3,128,512]{2,1,0:T(8,128)} %bitcast.4, bf16[16,256,512]{2,1,0:T(8,128)(2,1)} %constant.10.clone.tab_hbm, ...), custom_call_target="tpu_custom_call" | custom-call | tf_op jit(solution)/shard_map/misfit_adjoint/pallas_call | solution.py:452
  31.8 0.7 %copy.14 = f32[32,2048]{1,0:T(8,128)} copy(f32[32,2048]{1,0:T(8,128)S(1)} %get-tuple-element.6) | data formatting | bytes 524288
  32.5 0.5 %copy.15 = f32[128]{0:T(128)} copy(f32[128]{0:T(128)S(1)} %bitcast.3) | data formatting | bytes 1024

commit v5 on v4

--- a/solution.py
+++ b/solution.py
@@ -223,8 +223,8 @@
         return remote(fsend.at[rows], frecv.at[rows], (bfs_sem, bfr_sem), g, back(lax.rem(blk, 16) < 2))
 
     def late_grad(i):
-        rows = pl.ds(i * N1 // 2, N1 // 2), pl.ds(HALF, HALF)
-        return remote(fsend.at[rows], frecv.at[rows], (lbs_sem, lbr_sem), i, at(-2))
+        rows = pl.ds(12 * i, 12 - 8 * i), pl.ds(HALF, HALF)
+        return remote(fsend.at[rows], frecv.at[rows], (lbs_sem, lbr_sem), i, back(blk < 2) if i else at(-2))
 
     def swap(r):
         rows = pl.ds(16 * r, 16)
@@ -290,18 +290,15 @@
 
     loads["obs"].wait()
     loads["counts"].wait()
+    loads["tabt"].wait()
     slot = lax.broadcasted_iota(jnp.int32, (PAIRS, 1), 0)
     live = (slot < counts_ref[0]).astype(jnp.float32)
-    squares = jnp.zeros((PAIRS, 1), jnp.float32)
     for n in range(BANDS):
         rows = slice(PAIRS * n, PAIRS * (n + 1))
         residual = (corr[rows] - obs[n]) * live
-        squares = squares + jnp.sum(residual * residual, axis=1, keepdims=True)
         wgt[rows] = (residual * (1.0 / math.sqrt(FREQ_BINS / 8.0))).astype(jnp.bfloat16)
-    misfit = squares * (0.5 / (BANDS * LAGS))
-    mis_ref[...] = jnp.broadcast_to(misfit, (PAIRS, PAIRS)).T[0:1]
-
-    loads["tabt"].wait()
+        raw0[rows] = jnp.dot(wgt[rows], tabt[:, : 2 * F2 * PARTS[0][1]], preferred_element_type=jnp.float32)
+
 
     def lag_adjoint(g):
         lo, hi = PARTS[g]
@@ -314,7 +311,6 @@
         fsend[chunk(g)] = (far[chunk(g)] + nrecv[chunk(g)].astype(jnp.float32)).astype(jnp.bfloat16)
         far_grad(g).start()
 
-    lag_adjoint(0)
     for g, (lo, hi) in enumerate(PARTS):
         if 0 < g < CHUNKS - 1:
             lag_adjoint(g + 1)
@@ -357,6 +353,13 @@
     for i in range(2):
         late_grad(i).start()
 
+    squares = jnp.zeros((PAIRS, 1), jnp.float32)
+    for n in range(BANDS):
+        residual = (corr[PAIRS * n : PAIRS * (n + 1)] - obs[n]) * live
+        squares = squares + jnp.sum(residual * residual, axis=1, keepdims=True)
+    misfit = squares * (0.5 / (BANDS * LAGS))
+    mis_ref[...] = jnp.broadcast_to(misfit, (PAIRS, PAIRS)).T[0:1]
+
     loads["idft"].wait()
 
     @pl.when(odd == 0)
@@ -389,7 +392,7 @@
         else:
             for i in range(2):
                 late_grad(i).wait_recv()
-                invert(1, i * N1 // 2, (i + 1) * N1 // 2)
+                invert(1, 12 * i, 12 + 4 * i)
         total_e = jnp.zeros((16, 128), jnp.float32)
         total_w = jnp.zeros((16, 128), jnp.float32)
         for h in range(N2 // 128):

time: 33.1 us -> 32.8 us (level)
  the two profiles are of different devices: /device:TPU:7 before, /device:TPU:110 now
where the time goes in v5:
time: 32.8 us; the launch traced here: 32.7 us
  Pallas kernels  30.2 us (92%)
  between operations  1.28 us (4%)
  local copies, waits for them, and re-layouts  1.22 us (4%)
    pallas_call x1, Pallas kernels, per_device(): pl.pallas_call(kernel, out_shape=(pltpu.VMEM((CHAN, SAMPLES // 2), f32),...  30.2 us
    unnamed x2, local copies, waits for them, and re-layouts  1.22 us

profile of v5, /device:TPU:110, one launch (start us, length us, event | category | flops | bytes accessed | tf_op | source)
XLA Modules:
  0.0 32.7 jit_solution(9624814532258873119)
XLA Ops:
  1.3 30.2 %misfit_adjoint.1 = (f32[32,2048]{1,0:T(8,128)S(1)}, f32[1,128]{1,0:T(1,128)S(1)}) custom-call(bf16[32,4096]{1,0:T(8,128)(2,1)} %x_hbm.1, s32[2,128]{1,0:T(2,128)} %bitcast.5, s32[1]{0:T(128)S(6)} %copy.16.counts_hbm, s32[4]{0:T(128)} %edges_hbm.1, f32[3,128,512]{2,1,0:T(8,128)} %bitcast.4, bf16[16,256,512]{2,1,0:T(8,128)(2,1)} %constant.10.clone.tab_hbm, ...), custom_call_target="tpu_custom_call" | custom-call | tf_op jit(solution)/shard_map/misfit_adjoint/pallas_call | solution.py:455
  31.5 0.7 %copy.14 = f32[32,2048]{1,0:T(8,128)} copy(f32[32,2048]{1,0:T(8,128)S(1)} %get-tuple-element.6) | data formatting | bytes 524288
  32.2 0.5 %copy.15 = f32[128]{0:T(128)} copy(f32[128]{0:T(128)S(1)} %bitcast.3) | data formatting | bytes 1024

commit v6 on v5

--- a/solution.py
+++ b/solution.py
@@ -223,7 +223,7 @@
         return remote(fsend.at[rows], frecv.at[rows], (bfs_sem, bfr_sem), g, back(lax.rem(blk, 16) < 2))
 
     def late_grad(i):
-        rows = pl.ds(12 * i, 12 - 8 * i), pl.ds(HALF, HALF)
+        rows = pl.ds(14 * i, 14 - 12 * i), pl.ds(HALF, HALF)
         return remote(fsend.at[rows], frecv.at[rows], (lbs_sem, lbr_sem), i, back(blk < 2) if i else at(-2))
 
     def swap(r):
@@ -392,7 +392,7 @@
         else:
             for i in range(2):
                 late_grad(i).wait_recv()
-                invert(1, 12 * i, 12 + 4 * i)
+                invert(1, 14 * i, 14 + 2 * i)
         total_e = jnp.zeros((16, 128), jnp.float32)
         total_w = jnp.zeros((16, 128), jnp.float32)
         for h in range(N2 // 128):

time: 32.8 us -> 32.5 us (level)
  the two profiles are of different devices: /device:TPU:110 before, /device:TPU:7 now
where the time goes in v6:
time: 32.5 us; the launch traced here: 32.4 us
  Pallas kernels  29.9 us (92%)
  between operations  1.28 us (4%)
  local copies, waits for them, and re-layouts  1.22 us (4%)
    pallas_call x1, Pallas kernels, per_device(): pl.pallas_call(kernel, out_shape=(pltpu.VMEM((CHAN, SAMPLES // 2), f32),...  29.9 us
    unnamed x2, local copies, waits for them, and re-layouts  1.22 us

profile of v6, /device:TPU:7, one launch (start us, length us, event | category | flops | bytes accessed | tf_op | source)
XLA Modules:
  0.0 32.4 jit_solution(17743473405898535176)
XLA Ops:
  1.3 29.9 %misfit_adjoint.1 = (f32[32,2048]{1,0:T(8,128)S(1)}, f32[1,128]{1,0:T(1,128)S(1)}) custom-call(bf16[32,4096]{1,0:T(8,128)(2,1)} %x_hbm.1, s32[2,128]{1,0:T(2,128)} %bitcast.5, s32[1]{0:T(128)S(6)} %copy.16.counts_hbm, s32[4]{0:T(128)} %edges_hbm.1, f32[3,128,512]{2,1,0:T(8,128)} %bitcast.4, bf16[16,256,512]{2,1,0:T(8,128)(2,1)} %constant.10.clone.tab_hbm, ...), custom_call_target="tpu_custom_call" | custom-call | tf_op jit(solution)/shard_map/misfit_adjoint/pallas_call | solution.py:455
  31.1 0.7 %copy.14 = f32[32,2048]{1,0:T(8,128)} copy(f32[32,2048]{1,0:T(8,128)S(1)} %get-tuple-element.6) | data formatting | bytes 524288
  31.9 0.5 %copy.15 = f32[128]{0:T(128)} copy(f32[128]{0:T(128)S(1)} %bitcast.3) | data formatting | bytes 1024

commit v7 on v6

--- a/solution.py
+++ b/solution.py
@@ -223,7 +223,7 @@
         return remote(fsend.at[rows], frecv.at[rows], (bfs_sem, bfr_sem), g, back(lax.rem(blk, 16) < 2))
 
     def late_grad(i):
-        rows = pl.ds(14 * i, 14 - 12 * i), pl.ds(HALF, HALF)
+        rows = pl.ds(15 * i, 15 - 14 * i), pl.ds(HALF, HALF)
         return remote(fsend.at[rows], frecv.at[rows], (lbs_sem, lbr_sem), i, back(blk < 2) if i else at(-2))
 
     def swap(r):
@@ -392,7 +392,7 @@
         else:
             for i in range(2):
                 late_grad(i).wait_recv()
-                invert(1, 14 * i, 14 + 2 * i)
+                invert(1, 15 * i, 15 + i)
         total_e = jnp.zeros((16, 128), jnp.float32)
         total_w = jnp.zeros((16, 128), jnp.float32)
         for h in range(N2 // 128):

time: 32.5 us -> 32.7 us (level)
  no operation moved by 1% of the time
where the time goes in v7:
time: 32.7 us; the launch traced here: 32.5 us
  Pallas kernels  30 us (92%)
  between operations  1.28 us (4%)
  local copies, waits for them, and re-layouts  1.22 us (4%)
    pallas_call x1, Pallas kernels, per_device(): pl.pallas_call(kernel, out_shape=(pltpu.VMEM((CHAN, SAMPLES // 2), f32),...  30 us
    unnamed x2, local copies, waits for them, and re-layouts  1.22 us

profile of v7, /device:TPU:7, one launch (start us, length us, event | category | flops | bytes accessed | tf_op | source)
XLA Modules:
  0.0 32.5 jit_solution(428541887775274094)
XLA Ops:
  1.3 30.0 %misfit_adjoint.1 = (f32[32,2048]{1,0:T(8,128)S(1)}, f32[1,128]{1,0:T(1,128)S(1)}) custom-call(bf16[32,4096]{1,0:T(8,128)(2,1)} %x_hbm.1, s32[2,128]{1,0:T(2,128)} %bitcast.5, s32[1]{0:T(128)S(6)} %copy.16.counts_hbm, s32[4]{0:T(128)} %edges_hbm.1, f32[3,128,512]{2,1,0:T(8,128)} %bitcast.4, bf16[16,256,512]{2,1,0:T(8,128)(2,1)} %constant.10.clone.tab_hbm, ...), custom_call_target="tpu_custom_call" | custom-call | tf_op jit(solution)/shard_map/misfit_adjoint/pallas_call | solution.py:455
  31.3 0.7 %copy.14 = f32[32,2048]{1,0:T(8,128)} copy(f32[32,2048]{1,0:T(8,128)S(1)} %get-tuple-element.6) | data formatting | bytes 524288
  32.0 0.5 %copy.15 = f32[128]{0:T(128)} copy(f32[128]{0:T(128)S(1)} %bitcast.3) | data formatting | bytes 1024
